TPU v7x, 32 devices: a whole 2x2x4 slice. The times are simulated.
32 devices in a mesh: sec: 2 (over y), row: 4 (over x, core), col: 4 (over z).
Axes of the slice: x: 2, y: 2, z: 4, core: 2. Of those that a mesh axis runs over, the one named last changes fastest.
Arguments:
- pairs: float32 [2, 2, 2048, 4096], P('sec', None, 'row', 'col'), may hold values from -0.75 to 0.75
Outputs:
- combined: float32 [2, 2, 2048, 4096], P('sec', None, 'row', 'col')
All inputs are finite; a program needn't handle non-finite values.
Results may differ from a plain program's by a relative error of at most 0.0001.
Values sent between devices are 32-bit elements; how exact they have to be, the bound alone decides.
A program may use at most 128 MiB of HBM per device.

v0:
```python
import jax
import jax.numpy as jnp
from jax import lax
from jax.sharding import PartitionSpec as P


def from_partner(x, axis, stride):
    return lax.ppermute(x, axis, [(i, i ^ 1 << stride) for i in range(lax.axis_size(axis))])


def real_dot(left, right):
    return jnp.dot(left, right, precision=lax.Precision.HIGHEST, preferred_element_type=jnp.float32)


def real_form(columns):
    block_width = columns.shape[2] // 2
    blocks = columns.shape[1] // block_width
    shaped = columns.reshape(2, blocks, block_width, 2 * block_width)
    real_part = shaped[:, :, :, :block_width]
    imag_part = shaped[:, :, :, block_width:]
    lower = jnp.concatenate([-imag_part, real_part], axis=3)
    stacked = jnp.stack([shaped, lower], axis=2)
    return stacked.reshape(2, 2 * columns.shape[1], 2 * block_width)


def accumulate(block_piece, expanded):
    product = real_dot(block_piece[0], expanded[0])
    derivative = real_dot(block_piece[1], expanded[0]) + real_dot(block_piece[0], expanded[1])
    return (product, derivative)


def shards(pairs):
    own_pair = pairs[0]
    partner = from_partner(own_pair, "sec", 0)
    parity = lax.axis_index("sec") % 2
    first_pair = jnp.where(parity == 0, own_pair, partner)
    second_pair = jnp.where(parity == 0, partner, own_pair)
    columns = lax.all_gather(second_pair, "row", axis=1, tiled=True)
    expanded = real_form(columns)
    totals = accumulate(lax.all_gather(first_pair, "col", axis=2, tiled=True), expanded)
    combined = jnp.stack([totals[0], totals[1]])
    return combined[None]


def solution(mesh):
    placed = (P("sec", None, "row", "col"),)
    return jax.shard_map(
        shards, mesh=mesh, in_specs=placed, out_specs=P("sec", None, "row", "col"), check_vma=False
    )
```

profile of v0, /device:TPU:0, one launch (start us, length us, event | category | flops | bytes accessed | tf_op | source)
XLA Modules:
  0.0 608.2 jit_solution(11946845315793492560)
XLA Ops:
  6.5 0.0 all-gather.5.cloned.1.call-start
  6.5 3.0 collective-permute-start
  9.5 90.9 %collective-permute-done = f32[2,512,1024]{2,1,0:T(8,128)} collective-permute-done((f32[2,512,1024]{2,1,0:T(8,128)}, f32[2,512,1024]{2,1,0:T(8,128)}, u32[]{:S(2)}, u32[]{:S(2)}) %collective-permute-start) | collective-permute-done | bytes 4194336 | tf_op jit(solution)/shard_map/ppermute | solution.py:8
  100.4 8.8 %broadcast_select_fusion.1 = (f32[2,512,1024]{2,1,0:T(8,128)}, f32[2,512,1024]{2,1,0:T(8,128)}) fusion(f32[2,512,1024]{2,1,0:T(8,128)} %collective-permute-done, pred[]{:T(512)S(6)} %eq.6, f32[1,2,512,1024]{3,2,1,0:T(8,128)} %param.1), kind=kLoop, calls=%fused_computation.14 | loop fusion | flops 2097152 | bytes 16777216 | tf_op jit(solution)/shard_map/jit(_where)/select_n | solution.py:36
  109.2 0.0 all-gather.5.cloned.1.call-update
  109.3 0.0 all-gather.3.cloned.1.call-start
  109.3 0.7 all-gather.3.cloned.1.call-update
  110.0 106.8 %all-gather.5.cloned.1.call-done = f32[2,2048,1024]{2,1,0:T(8,128)} async-done(((f32[2,512,1024]{2,1,0:T(8,128)}), f32[2,2048,1024]{2,1,0:T(8,128)}) %all-gather.5.cloned.1.call-update) | async-done | bytes 16777232 | tf_op jit(solution)/shard_map/all_gather | solution.py:38
  216.8 0.0 slice-start
  216.8 0.0 slice-start.1
  216.8 13.5 %slice_negate_fusion = (f32[2,4,512,512]{3,2,1,0:T(8,128)}, f32[2,4,512,512]{3,2,1,0:T(8,128)}) fusion(f32[2,4,512,1024]{3,2,1,0:T(8,128)} %bitcast.29), kind=kLoop, calls=%fused_computation.7 | loop fusion | flops 2097152 | bytes 33554432 | tf_op jit(solution)/shard_map/neg | solution.py:21
  230.3 0.0 slice-start.2
  230.3 0.0 slice-start.3
  230.3 14.0 %maximum_bitcast_fusion = f32[2,4,1,512,1024]{4,3,2,1,0:T(8,128)} fusion(f32[2,4,512,512]{3,2,1,0:T(8,128)} %get-tuple-element.8, f32[2,4,512,512]{3,2,1,0:T(8,128)} %get-tuple-element.7), kind=kLoop, calls=%fused_computation.4 | loop fusion | flops 4194304 | bytes 33554432 | tf_op jit(solution)/shard_map/stack | solution.py:22
  244.3 0.0 slice-done
  244.3 0.0 slice-done.1
  244.3 0.0 slice-done.2
  244.3 0.7 slice-done.3
  245.1 17.5 %fusion = (f32[1,4,2,512,1024]{4,3,2,1,0:T(8,128)}, f32[1,4,2,512,1024]{4,3,2,1,0:T(8,128)}) fusion(f32[2,4,1,512,1024]{4,3,2,1,0:T(8,128)S(1)} %bitcast.32, f32[2,4,1,512,1024]{4,3,2,1,0:T(8,128)} %maximum_bitcast_fusion), kind=kLoop, calls=%fused_computation.2 | loop fusion | flops 8388608 | bytes 67108864 | tf_op jit(solution)/shard_map/stack | solution.py:22
  262.6 242.6 %all-gather.3.cloned.1.call-done = f32[2,512,4096]{2,1,0:T(8,128)} async-done(((f32[2,512,1024]{2,1,0:T(8,128)}), f32[2,512,4096]{2,1,0:T(8,128)}) %all-gather.3.cloned.1.call-update) | async-done | bytes 16777232 | tf_op jit(solution)/shard_map/all_gather | solution.py:40
  505.2 0.0 copy-start
  505.2 0.0 slice-start.4
  505.2 0.0 slice-start.5
  505.2 31.9 %fusion.4 = f32[1,512,1024]{2,1,0:T(8,128)} fusion(f32[4096,1024]{1,0:T(8,128)} %bitcast.33, f32[2,512,4096]{2,1,0:T(8,128)} %all-gather.3.cloned.1.call-done), kind=kOutput, calls=%fused_computation.15 | convolution fusion | flops 25769803776 | bytes 27262976 | tf_op jit(solution)/shard_map/dot_general | solution.py:12
  537.1 0.0 slice-start.6
  537.1 0.0 copy-done
  537.1 0.0 slice-start.7
  537.1 31.0 %fusion.2 = f32[512,1024]{1,0:T(8,128)} fusion(f32[4096,1024]{1,0:T(8,128)S(1)} %bitcast.37, f32[2,512,4096]{2,1,0:T(8,128)} %all-gather.3.cloned.1.call-done), kind=kOutput, calls=%fused_computation.9 | convolution fusion | flops 25769803776 | bytes 27262976 | tf_op jit(solution)/shard_map/dot_general | solution.py:12
  568.1 0.0 slice-done.4
  568.1 0.0 slice-done.5
  568.1 0.0 slice-done.6
  568.1 0.0 slice-done.7
  568.1 0.0 copy-start.1
  568.1 30.9 %add_bitcast_fusion = f32[1,512,1024]{2,1,0:T(8,128)S(1)} fusion(f32[512,1024]{1,0:T(8,128)} %fusion.2, f32[4096,1024]{1,0:T(8,128)S(1)} %bitcast.36, f32[2,512,4096]{2,1,0:T(8,128)} %all-gather.3.cloned.1.call-done), kind=kOutput, calls=%fused_computation.12 | convolution fusion | flops 25770328064 | bytes 29360128 | tf_op jit(solution)/shard_map/dot_general | solution.py:12
  599.0 0.0 copy-done.1
  599.0 2.3 maximum_bitcast_fusion.1
  (2 shorter events, 0.0 us)
Async XLA Ops:
  6.5 210.3 %all-gather.5.cloned.1.call-start = ((), (), s32[]{:S(2)}) async-start(), calls=%async_computation.1 | async-start | bytes 20971520 | tf_op jit(solution)/shard_map/all_gather | solution.py:38
  6.5 93.9 %collective-permute-start = (f32[2,512,1024]{2,1,0:T(8,128)}, f32[2,512,1024]{2,1,0:T(8,128)}, u32[]{:S(2)}, u32[]{:S(2)}) collective-permute-start(f32[2,512,1024]{2,1,0:T(8,128)} %bitcast.38), channel_id=1, source_target_pairs={{0,16},{16,0},{1,17},{17,1},{2,18},{18,2},{3,19},{19,3},{4,20},{20... | collective-permute-start | bytes 12582920 | tf_op jit(solution)/shard_map/ppermute | solution.py:8
  109.3 395.9 %all-gather.3.cloned.1.call-start = ((), (), s32[]{:S(2)}) async-start(), calls=%async_computation | async-start | bytes 20971520 | tf_op jit(solution)/shard_map/all_gather | solution.py:40
  216.8 27.5 %slice-start = ((s8[16777216]{0:T(1024)(128)(4,1)}), s8[4194304]{0:T(1024)(128)(4,1)S(1)}, s32[]{:S(2)}) async-start(s8[16777216]{0:T(1024)(128)(4,1)} %bitcast.30), calls=%async_computation.2 | async-start | bytes 8388608
  216.8 27.5 %slice-start.1 = ((s8[16777216]{0:T(1024)(128)(4,1)}), s8[4194304]{0:T(1024)(128)(4,1)S(1)}, s32[]{:S(2)}) async-start(s8[16777216]{0:T(1024)(128)(4,1)} %bitcast.30), calls=%async_computation.3 | async-start | bytes 8388608
  230.3 14.0 %slice-start.2 = ((s8[16777216]{0:T(1024)(128)(4,1)}), s8[4194304]{0:T(1024)(128)(4,1)S(1)}, s32[]{:S(2)}) async-start(s8[16777216]{0:T(1024)(128)(4,1)} %bitcast.30), calls=%async_computation.4 | async-start | bytes 8388608
  230.3 14.8 %slice-start.3 = ((s8[16777216]{0:T(1024)(128)(4,1)}), s8[4194304]{0:T(1024)(128)(4,1)S(1)}, s32[]{:S(2)}) async-start(s8[16777216]{0:T(1024)(128)(4,1)} %bitcast.30), calls=%async_computation.5 | async-start | bytes 8388608
  505.2 31.9 %copy-start = (f32[1,4,2,512,1024]{4,3,2,1,0:T(8,128)S(1)}, f32[1,4,2,512,1024]{4,3,2,1,0:T(8,128)}, u32[]{:S(2)}) copy-start(f32[1,4,2,512,1024]{4,3,2,1,0:T(8,128)} %get-tuple-element.6) | copy-start | bytes 50331652
  505.2 62.9 %slice-start.4 = ((s8[16777216]{0:T(1024)(128)(4,1)}), s8[4194304]{0:T(1024)(128)(4,1)S(1)}, s32[]{:S(2)}) async-start(s8[16777216]{0:T(1024)(128)(4,1)} %bitcast.34), calls=%async_computation.6 | async-start | bytes 8388608
  505.2 62.9 %slice-start.5 = ((s8[16777216]{0:T(1024)(128)(4,1)}), s8[4194304]{0:T(1024)(128)(4,1)S(1)}, s32[]{:S(2)}) async-start(s8[16777216]{0:T(1024)(128)(4,1)} %bitcast.34), calls=%async_computation.7 | async-start | bytes 8388608
  537.1 31.0 %slice-start.6 = ((s8[16777216]{0:T(1024)(128)(4,1)}), s8[4194304]{0:T(1024)(128)(4,1)S(1)}, s32[]{:S(2)}) async-start(s8[16777216]{0:T(1024)(128)(4,1)} %bitcast.34), calls=%async_computation.8 | async-start | bytes 8388608
  537.1 31.0 %slice-start.7 = ((s8[16777216]{0:T(1024)(128)(4,1)}), s8[4194304]{0:T(1024)(128)(4,1)S(1)}, s32[]{:S(2)}) async-start(s8[16777216]{0:T(1024)(128)(4,1)} %bitcast.34), calls=%async_computation.9 | async-start | bytes 8388608
  568.1 30.9 %copy-start.1 = (f32[1,512,1024]{2,1,0:T(8,128)S(1)}, f32[1,512,1024]{2,1,0:T(8,128)}, u32[]{:S(2)}) copy-start(f32[1,512,1024]{2,1,0:T(8,128)} %fusion.4) | copy-start | bytes 6291460
Sparse Core Ops, SparseCore 0:
  109.4 107.3 all-gather.4
  218.4 286.7 all-gather.2
where the time goes:
time: 608 us
  waiting for transfers between devices  441 us (73%)
  matrix products  93.8 us (15%)
  other arithmetic  56.2 us (9%)
  between operations  13.5 us (2%)
    all_gather x1, waiting for transfers between devices, shards(): lax.all_gather(first_pair, 'col', axis=2, tiled=True)  243 us
    all_gather x1, waiting for transfers between devices, shards(): columns = lax.all_gather(second_pair, 'row', axis=1, tiled=True)  107 us
    dot_general x3, matrix products, real_dot(): jnp.dot(left, right, precision=lax.Precision.HIGHEST, preferred_element_t...  93.8 us
    ppermute x1, waiting for transfers between devices, from_partner(): lax.ppermute(x, axis, [(i, i ^ 1 << stride) for i in range(lax.axis_size(...  90.9 us
    another operation x2, other arithmetic, real_form(): stacked = jnp.stack([shaped, lower], axis=2)  31.5 us
    neg x1, other arithmetic, real_form(): lower = jnp.concatenate([-imag_part, real_part], axis=3)  13.5 us
  transfers between devices with their start and end apart: 3, of which 3 were waited for; matrix products, arithmetic and copies ran while one was open for 7% of the time, Pallas kernels for 0%

commit v1 on v0

v1 whole, which is shorter than its diff:
```python
import functools

import jax
import jax.numpy as jnp
from jax import lax
from jax.experimental import pallas as pl
from jax.experimental.pallas import tpu as pltpu
from jax.sharding import PartitionSpec as P

MESH = pl.DeviceIdType.MESH
ROW_CHUNKS = 4
B_CHUNKS = 8


def split(x):
    hi = x.astype(jnp.bfloat16)
    lo = (x - hi.astype(jnp.float32)).astype(jnp.bfloat16)
    return hi, lo


def kernel(
    n_col, x_ref, o_ref, a_land, b_land, b_hi, b_lo, lhs, acc, out_v,
    a_recv, a_right, a_left, ya_send, b_recv, yb_send, b_send, out_sem,
):
    T, U = ROW_CHUNKS, B_CHUNKS
    rows, width = x_ref.shape[1], x_ref.shape[2]
    half = rows // 2
    mt = half // T
    ub = rows // U
    kw = width // 2
    tile = 256

    sec, row, col = lax.axis_index("sec"), lax.axis_index("row"), lax.axis_index("col")
    parity = lax.rem(sec, 2)
    partner = {"sec": sec + 1 - 2 * parity}
    row1 = row + 1 - 2 * lax.rem(row, 2)
    row2 = row + 2 - 4 * lax.rem(lax.div(row, 2), 2)
    row3 = row1 + row2 - row
    has_left, has_right = col > 0, col < n_col - 1

    def remote(src, dst, send, recv, device):
        return pltpu.make_async_remote_copy(
            src_ref=src, dst_ref=dst, send_sem=send, recv_sem=recv,
            device_id=device, device_id_type=MESH,
        )

    def a_slot(j, t):
        return a_land.at[j, t]

    def a_rows(t, base):
        return x_ref.at[:, pl.ds(base + t * mt, mt), :]

    def b_slot(who, u):
        return b_land.at[:, pl.ds(pl.multiple_of(who * rows + u * ub, ub), ub), :]

    def right_copy(j, t):
        return remote(a_slot(j, t), a_slot(j, t), a_right.at[j, t], a_recv.at[j, t], {"col": col + 1})

    def left_copy(j, t):
        return remote(a_slot(j, t), a_slot(j, t), a_left.at[j, t], a_recv.at[j, t], {"col": col - 1})

    def ya_copy(t):
        return remote(a_rows(t, half), a_slot(col, t), ya_send.at[t], a_recv.at[col, t], partner)

    def yb_copy(u):
        return remote(
            x_ref.at[:, pl.ds(u * ub, ub), :], b_slot(row, u), yb_send.at[u], b_recv.at[0, u], partner
        )

    def b_copy(kind, u):
        who = row2 if kind == 2 else row
        device = {"row": row2} if kind == 1 else {"row": row1}
        return remote(
            b_slot(who, u), b_slot(who, u), b_send.at[kind, u], b_recv.at[kind + 1, u], device
        )

    def b_wait(kind, who, u):
        pltpu.make_async_copy(b_slot(who, u), b_slot(who, u), b_recv.at[kind, u]).wait()

    def convert(who, u):
        step = 16

        @pl.loop(0, ub // step)
        def _(i):
            at = pl.ds(pl.multiple_of(who * rows + u * ub + i * step, step), step)
            hi, lo = split(b_land[:, at, :])
            b_hi[:, at, :] = hi
            b_lo[:, at, :] = lo

    def handle(j, t):
        pltpu.make_async_copy(a_slot(j, t), a_slot(j, t), a_recv.at[j, t]).wait()

        @pl.when(jnp.logical_and(j <= col, has_right))
        def _():
            right_copy(j, t).start()

        @pl.when(jnp.logical_and(j >= col, has_left))
        def _():
            left_copy(j, t).start()

    def a_tick(t, d):
        @pl.when(col >= d)
        def _():
            handle(col - d, t)

        @pl.when(col + d < n_col)
        def _():
            handle(col + d, t)

    def unit(j, t):
        for mat in range(2):
            for part in range(2):
                at = pl.ds((2 * mat + part) * mt, mt)
                hi, lo = split(a_land[j, t, mat, :, part * kw:(part + 1) * kw])
                lhs[at, 0:kw] = hi
                lhs[at, kw:2 * kw] = hi
                lhs[at, 2 * kw:3 * kw] = lo
        depth = pl.ds(pl.multiple_of(j * kw, kw), kw)

        @pl.loop(0, width // tile)
        def _(n):
            cols = pl.ds(pl.multiple_of(n * tile, tile), tile)
            rhs = []
            for mat in range(2):
                hi, lo = b_hi[mat, depth, cols], b_lo[mat, depth, cols]
                rhs.append(jnp.concatenate([hi, lo, hi], axis=0))
            acc[:, cols] += jnp.dot(lhs[...], rhs[0], preferred_element_type=jnp.float32)
            acc[2 * mt:4 * mt, cols] += jnp.dot(
                lhs[0:2 * mt, :], rhs[1], preferred_element_type=jnp.float32
            )

    def out_rows(t, base):
        return o_ref.at[:, pl.ds(pl.multiple_of(base + t * mt, mt), mt), :]

    def out_remote(t):
        return remote(
            out_v.at[t], out_rows(t, parity * half), out_sem.at[0, t], out_sem.at[1, t], partner
        )

    def out_local(t):
        return pltpu.make_async_copy(out_v.at[t], out_rows(t, parity * half), out_sem.at[2, t])

    def finish(t):
        for mat in range(2):
            p = acc[2 * mat * mt:(2 * mat + 1) * mt, :]
            q = acc[(2 * mat + 1) * mt:(2 * mat + 2) * mt, :]
            out_v[t, mat, :, 0:kw] = p[:, 0:kw] - q[:, kw:]
            out_v[t, mat, :, kw:] = p[:, kw:] + q[:, 0:kw]
        out_remote(t).start()
        out_local(t).start()

    barrier = pltpu.get_barrier_semaphore()
    for device in (partner, {"row": row1}, {"row": row2}):
        pl.semaphore_signal(barrier, inc=1, device_id=device, device_id_type=MESH)

    @pl.when(has_left)
    def _():
        pl.semaphore_signal(barrier, inc=1, device_id={"col": col - 1}, device_id_type=MESH)

    @pl.when(has_right)
    def _():
        pl.semaphore_signal(barrier, inc=1, device_id={"col": col + 1}, device_id_type=MESH)

    pl.semaphore_wait(barrier, 3 + has_left.astype(jnp.int32) + has_right.astype(jnp.int32))

    @pl.when(parity == 0)
    def _():
        for t in range(T):
            if t < 2:
                ya_copy(t).start()
            pltpu.make_async_copy(a_rows(t, 0), a_slot(col, t), a_recv.at[col, t]).start()

    @pl.when(parity == 1)
    def _():
        for u in range(U):
            if u < 2:
                yb_copy(u).start()
            pltpu.make_async_copy(
                x_ref.at[:, pl.ds(u * ub, ub), :], b_slot(row, u), b_recv.at[0, u]
            ).start()

    per_chunk = n_col - 1
    a_ticks = (T - 1) * per_chunk
    for tick in range(max(a_ticks, U + 2)):
        if tick == 0:
            handle(col, 0)
        if tick < U:
            b_wait(0, row, tick)
            b_copy(1, tick).start()
            b_copy(0, tick).start()
            convert(row, tick)
        if tick < a_ticks:
            t, d = tick // per_chunk, tick % per_chunk + 1
            a_tick(t, d)
            if d == max(per_chunk - 1, 1):
                handle(col, t + 1)
        if 1 <= tick < U + 1:
            b_wait(2, row2, tick - 1)
            b_copy(2, tick - 1).start()
            b_wait(1, row1, tick - 1)
            convert(row2, tick - 1)
            convert(row1, tick - 1)
        if 2 <= tick < U + 2:
            b_wait(3, row3, tick - 2)
            convert(row3, tick - 2)
        if tick + 2 < U:
            @pl.when(parity == 1)
            def _():
                yb_copy(tick).wait_send()
                yb_copy(tick + 2).start()
        if tick + 2 < T:
            @pl.when(parity == 0)
            def _():
                ya_copy(tick).wait_send()
                ya_copy(tick + 2).start()

    given = 0
    for t in range(T - 1):
        acc[...] = jnp.zeros_like(acc)

        @pl.loop(0, n_col)
        def _(j):
            unit(j, t)

        finish(t)
        due = per_chunk * (t + 1) // (T - 1) if t < T - 2 else per_chunk
        if t < T - 2:
            for d in range(given + 1, due + 1):
                a_tick(T - 1, d)
            given = due

    acc[...] = jnp.zeros_like(acc)
    unit(col, T - 1)

    @pl.loop(1, n_col)
    def _(d):
        for j, there in ((col - d, col >= d), (col + d, col + d < n_col)):
            @pl.when(there)
            def _():
                @pl.when(d > given)
                def _():
                    handle(j, T - 1)

                unit(j, T - 1)

    finish(T - 1)

    for t in range(T):
        out_local(t).wait()
        out_remote(t).wait_send()
        pltpu.make_async_copy(
            out_v.at[t], out_rows(t, (1 - parity) * half), out_sem.at[1, t]
        ).wait()

    for kind in range(3):
        for u in range(U):
            b_copy(kind, u).wait_send()

    @pl.when(parity == 0)
    def _():
        for t in range(max(T - 2, 0), T):
            ya_copy(t).wait_send()

    @pl.when(parity == 1)
    def _():
        for u in range(max(U - 2, 0), U):
            yb_copy(u).wait_send()

    @pl.loop(0, n_col)
    def _(j):
        @pl.when(jnp.logical_and(j <= col, has_right))
        def _():
            for t in range(T):
                right_copy(j, t).wait_send()

        @pl.when(jnp.logical_and(j >= col, has_left))
        def _():
            for t in range(T):
                left_copy(j, t).wait_send()


def shards(n_row, n_col, pairs):
    _, _, rows, width = pairs.shape
    T, U = ROW_CHUNKS, B_CHUNKS
    mt = rows // 2 // T
    dma = pltpu.SemaphoreType.DMA
    combined = pl.pallas_call(
        functools.partial(kernel, n_col),
        out_shape=jax.ShapeDtypeStruct((2, rows, width), jnp.float32),
        in_specs=[pl.BlockSpec(memory_space=pl.ANY)],
        out_specs=pl.BlockSpec(memory_space=pl.ANY),
        scratch_shapes=[
            pltpu.VMEM((n_col, T, 2, mt, width), jnp.float32),
            pltpu.VMEM((2, n_row * rows, width), jnp.float32),
            pltpu.VMEM((2, n_row * rows, width), jnp.bfloat16),
            pltpu.VMEM((2, n_row * rows, width), jnp.bfloat16),
            pltpu.VMEM((4 * mt, 3 * width // 2), jnp.bfloat16),
            pltpu.VMEM((4 * mt, width), jnp.float32),
            pltpu.VMEM((T, 2, mt, width), jnp.float32),
            dma((n_col, T)),
            dma((n_col, T)),
            dma((n_col, T)),
            dma((T,)),
            dma((4, U)),
            dma((U,)),
            dma((3, U)),
            dma((3, T)),
        ],
        compiler_params=pltpu.CompilerParams(
            collective_id=0, has_side_effects=True, vmem_limit_bytes=58 * 1024 * 1024
        ),
    )(pairs[0])
    return combined[None]


def solution(mesh):
    spec = P("sec", None, "row", "col")
    return jax.shard_map(
        functools.partial(shards, mesh.shape["row"], mesh.shape["col"]),
        mesh=mesh, in_specs=(spec,), out_specs=spec, check_vma=False,
    )
```

time: 608 us -> 184 us (0.30)
  waiting for transfers between devices: 441 us -> 0 us
  Pallas kernels: 0 us -> 179 us
  matrix products: 93.8 us -> 0 us
  other arithmetic: 56.2 us -> 0 us
  between operations: 13.5 us -> 0.01 us
    all_gather x2 -> x0, waiting for transfers between devices: 349 us -> none  [the longest x1 243 us: shards(): lax.all_gather(first_pair, 'col', axis=2, tiled=True)]
    pallas_call x0 -> x1, Pallas kernels: none -> 179 us  [shards(): pl.pallas_call(functools.partial(kernel, n_col), out_shape=jax.ShapeDtype...]
    dot_general x3 -> x0, matrix products: 93.8 us -> none  [real_dot(): jnp.dot(left, right, precision=lax.Precision.HIGHEST, preferred_element_t...]
    ppermute x1 -> x0, waiting for transfers between devices: 90.9 us -> none  [from_partner(): lax.ppermute(x, axis, [(i, i ^ 1 << stride) for i in range(lax.axis_size(...]
    another operation x2 -> x0, other arithmetic: 31.5 us -> none  [real_form(): stacked = jnp.stack([shaped, lower], axis=2)]
    neg x1 -> x0, other arithmetic: 13.5 us -> none  [real_form(): lower = jnp.concatenate([-imag_part, real_part], axis=3)]
    select_n x1 -> x0, other arithmetic: 8.84 us -> none  [shards(): first_pair = jnp.where(parity == 0, own_pair, partner)]
  transfers between devices with their start and end apart: 3 -> 0, of which waited for: 3 -> 0; matrix products, arithmetic and copies ran while one was open for 7% -> 0% of each run, Pallas kernels for 0% -> 0%
where the time goes in v1:
time: 184 us
  Pallas kernels  179 us (97%)
  local copies, waits for them, and re-layouts  4.79 us (3%)
    pallas_call x1, Pallas kernels, shards(): pl.pallas_call(functools.partial(kernel, n_col), out_shape=jax.ShapeDtype...  179 us
    unnamed x1, local copies, waits for them, and re-layouts  4.79 us

profile of v1, /device:TPU:0, one launch (start us, length us, event | category | flops | bytes accessed | tf_op | source)
XLA Modules:
  0.0 184.2 jit_solution(16301164639465297188)
XLA Ops:
  0.0 179.4 %shard_map.17 = f32[2,512,1024]{2,1,0:T(8,128)} custom-call(f32[2,512,1024]{2,1,0:T(8,128)} %bitcast.3), custom_call_target="tpu_custom_call" | custom-call | tf_op jit(solution)/shard_map/pallas_call | solution.py:287
  179.4 4.8 %copy.3 = f32[1,2,512,1024]{3,2,1,0:T(8,128)} copy(f32[1,2,512,1024]{3,2,1,0:T(8,128)} %bitcast.2) | data formatting | bytes 8388608

commit v2 on v1

--- a/solution.py
+++ b/solution.py
@@ -107,27 +107,31 @@
         def _():
             handle(col + d, t)
 
-    def unit(j, t):
+    def unit(j, t, k0, depth):
         for mat in range(2):
             for part in range(2):
                 at = pl.ds((2 * mat + part) * mt, mt)
-                hi, lo = split(a_land[j, t, mat, :, part * kw:(part + 1) * kw])
-                lhs[at, 0:kw] = hi
-                lhs[at, kw:2 * kw] = hi
-                lhs[at, 2 * kw:3 * kw] = lo
-        depth = pl.ds(pl.multiple_of(j * kw, kw), kw)
+                first = part * kw + k0
+                hi, lo = split(a_land[j, t, mat, :, first:first + depth])
+                lhs[at, 0:depth] = hi
+                lhs[at, depth:2 * depth] = hi
+                lhs[at, 2 * depth:3 * depth] = lo
+        deep = pl.ds(pl.multiple_of(j * kw + k0, depth), depth)
+        here = pl.ds(pl.multiple_of(t * mt, mt), mt)
 
         @pl.loop(0, width // tile)
         def _(n):
             cols = pl.ds(pl.multiple_of(n * tile, tile), tile)
             rhs = []
             for mat in range(2):
-                hi, lo = b_hi[mat, depth, cols], b_lo[mat, depth, cols]
+                hi, lo = b_hi[mat, deep, cols], b_lo[mat, deep, cols]
                 rhs.append(jnp.concatenate([hi, lo, hi], axis=0))
-            acc[:, cols] += jnp.dot(lhs[...], rhs[0], preferred_element_type=jnp.float32)
-            acc[2 * mt:4 * mt, cols] += jnp.dot(
-                lhs[0:2 * mt, :], rhs[1], preferred_element_type=jnp.float32
+            both = jnp.dot(lhs[:, 0:3 * depth], rhs[0], preferred_element_type=jnp.float32)
+            cross = jnp.dot(
+                lhs[0:2 * mt, 0:3 * depth], rhs[1], preferred_element_type=jnp.float32
             )
+            acc[0:2, here, cols] += both[0:2 * mt].reshape(2, mt, tile)
+            acc[2:4, here, cols] += (both[2 * mt:] + cross).reshape(2, mt, tile)
 
     def out_rows(t, base):
         return o_ref.at[:, pl.ds(pl.multiple_of(base + t * mt, mt), mt), :]
@@ -141,9 +145,10 @@
         return pltpu.make_async_copy(out_v.at[t], out_rows(t, parity * half), out_sem.at[2, t])
 
     def finish(t):
+        here = pl.ds(pl.multiple_of(t * mt, mt), mt)
         for mat in range(2):
-            p = acc[2 * mat * mt:(2 * mat + 1) * mt, :]
-            q = acc[(2 * mat + 1) * mt:(2 * mat + 2) * mt, :]
+            p = acc[2 * mat, here, :]
+            q = acc[2 * mat + 1, here, :]
             out_v[t, mat, :, 0:kw] = p[:, 0:kw] - q[:, kw:]
             out_v[t, mat, :, kw:] = p[:, kw:] + q[:, 0:kw]
         out_remote(t).start()
@@ -173,77 +178,87 @@
     @pl.when(parity == 1)
     def _():
         for u in range(U):
-            if u < 2:
+            if u < 3:
                 yb_copy(u).start()
             pltpu.make_async_copy(
                 x_ref.at[:, pl.ds(u * ub, ub), :], b_slot(row, u), b_recv.at[0, u]
             ).start()
 
-    per_chunk = n_col - 1
-    a_ticks = (T - 1) * per_chunk
-    for tick in range(max(a_ticks, U + 2)):
-        if tick == 0:
-            handle(col, 0)
+    last = n_col - 1
+    a_ticks = (last - 1) * T
+    early = {U // 2 + 1: 0, U // 2 + 2: 1, 2 * T: 2} if kw == rows and n_col == 4 else {}
+
+    @pl.when(parity == 0)
+    def _():
+        handle(col, 0)
+
+    acc[...] = jnp.zeros_like(acc)
+    for tick in range(max(a_ticks + 1, U + 2)):
         if tick < U:
             b_wait(0, row, tick)
             b_copy(1, tick).start()
             b_copy(0, tick).start()
-            convert(row, tick)
-        if tick < a_ticks:
-            t, d = tick // per_chunk, tick % per_chunk + 1
-            a_tick(t, d)
-            if d == max(per_chunk - 1, 1):
-                handle(col, t + 1)
+        if tick < T:
+            @pl.when(parity == 1)
+            def _():
+                handle(col, tick)
+        if tick + 1 < T:
+            @pl.when(parity == 0)
+            def _():
+                handle(col, tick + 1)
+        if 1 <= tick < a_ticks + 1:
+            a_tick((tick - 1) % T, (tick - 1) // T + 1)
         if 1 <= tick < U + 1:
             b_wait(2, row2, tick - 1)
             b_copy(2, tick - 1).start()
+        if tick + 3 < U:
+            @pl.when(parity == 1)
+            def _():
+                yb_copy(tick).wait_send()
+                yb_copy(tick + 3).start()
+        if tick + 2 < T:
+            @pl.when(parity == 0)
+            def _():
+                ya_copy(tick).wait_send()
+                ya_copy(tick + 2).start()
+        if tick < U:
+            convert(row, tick)
+        if 1 <= tick < U + 1:
             b_wait(1, row1, tick - 1)
+            convert(row1, tick - 1)
             convert(row2, tick - 1)
-            convert(row1, tick - 1)
         if 2 <= tick < U + 2:
             b_wait(3, row3, tick - 2)
             convert(row3, tick - 2)
-        if tick + 2 < U:
-            @pl.when(parity == 1)
-            def _():
-                yb_copy(tick).wait_send()
-                yb_copy(tick + 2).start()
-        if tick + 2 < T:
-            @pl.when(parity == 0)
-            def _():
-                ya_copy(tick).wait_send()
-                ya_copy(tick + 2).start()
-
-    given = 0
-    for t in range(T - 1):
-        acc[...] = jnp.zeros_like(acc)
-
-        @pl.loop(0, n_col)
-        def _(j):
-            unit(j, t)
+        if tick in early:
+            dist = early[tick]
+
+            @pl.loop(0, T * (2 if dist else 1))
+            def _(i):
+                j = col + dist * (1 - 2 * lax.div(i, T))
+
+                @pl.when(jnp.logical_and(j >= 0, j < n_col))
+                def _():
+                    unit(j, lax.rem(i, T), 0, kw // 2)
+
+    k0 = kw // 2 if early else 0
+
+    @pl.loop(0, T)
+    def _(t):
+        @pl.loop(0, 2 * last - 1)
+        def _(i):
+            j = col + lax.div(i + 1, 2) * (1 - 2 * lax.rem(i, 2))
+
+            @pl.when(jnp.logical_and(j >= 0, j < n_col))
+            def _():
+                unit(j, t, k0, kw - k0)
+
+        @pl.when(jnp.logical_or(col == 0, col == last))
+        def _():
+            handle(last - col, t)
+            unit(last - col, t, 0, kw)
 
         finish(t)
-        due = per_chunk * (t + 1) // (T - 1) if t < T - 2 else per_chunk
-        if t < T - 2:
-            for d in range(given + 1, due + 1):
-                a_tick(T - 1, d)
-            given = due
-
-    acc[...] = jnp.zeros_like(acc)
-    unit(col, T - 1)
-
-    @pl.loop(1, n_col)
-    def _(d):
-        for j, there in ((col - d, col >= d), (col + d, col + d < n_col)):
-            @pl.when(there)
-            def _():
-                @pl.when(d > given)
-                def _():
-                    handle(j, T - 1)
-
-                unit(j, T - 1)
-
-    finish(T - 1)
 
     for t in range(T):
         out_local(t).wait()
@@ -263,7 +278,7 @@
 
     @pl.when(parity == 1)
     def _():
-        for u in range(max(U - 2, 0), U):
+        for u in range(max(U - 3, 0), U):
             yb_copy(u).wait_send()
 
     @pl.loop(0, n_col)
@@ -295,7 +310,7 @@
             pltpu.VMEM((2, n_row * rows, width), jnp.bfloat16),
             pltpu.VMEM((2, n_row * rows, width), jnp.bfloat16),
             pltpu.VMEM((4 * mt, 3 * width // 2), jnp.bfloat16),
-            pltpu.VMEM((4 * mt, width), jnp.float32),
+            pltpu.VMEM((4, rows // 2, width), jnp.float32),
             pltpu.VMEM((T, 2, mt, width), jnp.float32),
             dma((n_col, T)),
             dma((n_col, T)),

time: 184 us -> 185 us (level)
  no operation moved by 1% of the time
where the time goes in v2:
time: 185 us
  Pallas kernels  180 us (97%)
  local copies, waits for them, and re-layouts  4.79 us (3%)
    pallas_call x1, Pallas kernels, shards(): pl.pallas_call(functools.partial(kernel, n_col), out_shape=jax.ShapeDtype...  180 us
    unnamed x1, local copies, waits for them, and re-layouts  4.79 us

profile of v2, /device:TPU:0, one launch (start us, length us, event | category | flops | bytes accessed | tf_op | source)
XLA Modules:
  0.0 185.0 jit_solution(12475507308266574910)
XLA Ops:
  0.0 180.2 %shard_map.17 = f32[2,512,1024]{2,1,0:T(8,128)} custom-call(f32[2,512,1024]{2,1,0:T(8,128)} %bitcast.3), custom_call_target="tpu_custom_call" | custom-call | tf_op jit(solution)/shard_map/pallas_call | solution.py:302
  180.2 4.8 %copy.3 = f32[1,2,512,1024]{3,2,1,0:T(8,128)} copy(f32[1,2,512,1024]{3,2,1,0:T(8,128)} %bitcast.2) | data formatting | bytes 8388608

commit v3 on v2

--- a/solution.py
+++ b/solution.py
@@ -107,31 +107,35 @@
         def _():
             handle(col + d, t)
 
-    def unit(j, t, k0, depth):
+    def unit(j, t, n, k0, depth):
+        m = n * mt
         for mat in range(2):
             for part in range(2):
-                at = pl.ds((2 * mat + part) * mt, mt)
+                at = pl.ds((2 * mat + part) * m, m)
                 first = part * kw + k0
-                hi, lo = split(a_land[j, t, mat, :, first:first + depth])
+                x = a_land[j, pl.ds(t, n), mat, :, first:first + depth]
+                hi, lo = split(x.reshape(m, depth))
                 lhs[at, 0:depth] = hi
                 lhs[at, depth:2 * depth] = hi
                 lhs[at, 2 * depth:3 * depth] = lo
         deep = pl.ds(pl.multiple_of(j * kw + k0, depth), depth)
-        here = pl.ds(pl.multiple_of(t * mt, mt), mt)
+        here = pl.ds(pl.multiple_of(t * mt, mt), m)
 
         @pl.loop(0, width // tile)
-        def _(n):
-            cols = pl.ds(pl.multiple_of(n * tile, tile), tile)
+        def _(c):
+            cols = pl.ds(pl.multiple_of(c * tile, tile), tile)
             rhs = []
             for mat in range(2):
                 hi, lo = b_hi[mat, deep, cols], b_lo[mat, deep, cols]
                 rhs.append(jnp.concatenate([hi, lo, hi], axis=0))
-            both = jnp.dot(lhs[:, 0:3 * depth], rhs[0], preferred_element_type=jnp.float32)
+            both = jnp.dot(
+                lhs[0:4 * m, 0:3 * depth], rhs[0], preferred_element_type=jnp.float32
+            )
+            acc[0:4, here, cols] += both.reshape(4, m, tile)
             cross = jnp.dot(
-                lhs[0:2 * mt, 0:3 * depth], rhs[1], preferred_element_type=jnp.float32
+                lhs[0:2 * m, 0:3 * depth], rhs[1], preferred_element_type=jnp.float32
             )
-            acc[0:2, here, cols] += both[0:2 * mt].reshape(2, mt, tile)
-            acc[2:4, here, cols] += (both[2 * mt:] + cross).reshape(2, mt, tile)
+            acc[2:4, here, cols] += cross.reshape(2, m, tile)
 
     def out_rows(t, base):
         return o_ref.at[:, pl.ds(pl.multiple_of(base + t * mt, mt), mt), :]
@@ -186,7 +190,7 @@
 
     last = n_col - 1
     a_ticks = (last - 1) * T
-    early = {U // 2 + 1: 0, U // 2 + 2: 1, 2 * T: 2} if kw == rows and n_col == 4 else {}
+    early = {5: (0, 0), 6: (-1, -1), 7: (1, 1), 8: (-2, 2)} if kw == rows and n_col == 4 else {}
 
     @pl.when(parity == 0)
     def _():
@@ -231,34 +235,35 @@
             b_wait(3, row3, tick - 2)
             convert(row3, tick - 2)
         if tick in early:
-            dist = early[tick]
-
-            @pl.loop(0, T * (2 if dist else 1))
-            def _(i):
-                j = col + dist * (1 - 2 * lax.div(i, T))
-
-                @pl.when(jnp.logical_and(j >= 0, j < n_col))
-                def _():
-                    unit(j, lax.rem(i, T), 0, kw // 2)
+            down, up = early[tick]
+            j = jnp.where(col + down >= 0, col + down, col + up)
+
+            @pl.when(jnp.logical_and(j >= 0, j < n_col))
+            def _():
+                @pl.loop(0, T // 2)
+                def _(p):
+                    unit(j, 2 * p, 2, 0, kw // 2)
 
     k0 = kw // 2 if early else 0
 
-    @pl.loop(0, T)
-    def _(t):
+    @pl.loop(0, T // 2)
+    def _(p):
         @pl.loop(0, 2 * last - 1)
         def _(i):
             j = col + lax.div(i + 1, 2) * (1 - 2 * lax.rem(i, 2))
 
             @pl.when(jnp.logical_and(j >= 0, j < n_col))
             def _():
-                unit(j, t, k0, kw - k0)
-
-        @pl.when(jnp.logical_or(col == 0, col == last))
-        def _():
-            handle(last - col, t)
-            unit(last - col, t, 0, kw)
-
-        finish(t)
+                unit(j, 2 * p, 2, k0, kw - k0)
+
+        @pl.loop(2 * p, 2 * p + 2)
+        def _(t):
+            @pl.when(jnp.logical_or(col == 0, col == last))
+            def _():
+                handle(last - col, t)
+                unit(last - col, t, 1, 0, kw)
+
+            finish(t)
 
     for t in range(T):
         out_local(t).wait()
@@ -309,7 +314,7 @@
             pltpu.VMEM((2, n_row * rows, width), jnp.float32),
             pltpu.VMEM((2, n_row * rows, width), jnp.bfloat16),
             pltpu.VMEM((2, n_row * rows, width), jnp.bfloat16),
-            pltpu.VMEM((4 * mt, 3 * width // 2), jnp.bfloat16),
+            pltpu.VMEM((8 * mt, 3 * width // 2), jnp.bfloat16),
             pltpu.VMEM((4, rows // 2, width), jnp.float32),
             pltpu.VMEM((T, 2, mt, width), jnp.float32),
             dma((n_col, T)),

time: 185 us -> 184 us (level)
  no operation moved by 1% of the time
where the time goes in v3:
time: 184 us
  Pallas kernels  179 us (97%)
  local copies, waits for them, and re-layouts  4.79 us (3%)
    pallas_call x1, Pallas kernels, shards(): pl.pallas_call(functools.partial(kernel, n_col), out_shape=jax.ShapeDtype...  179 us
    unnamed x1, local copies, waits for them, and re-layouts  4.79 us

profile of v3, /device:TPU:0, one launch (start us, length us, event | category | flops | bytes accessed | tf_op | source)
XLA Modules:
  0.0 184.0 jit_solution(6134209131525126858)
XLA Ops:
  0.0 179.2 %shard_map.17 = f32[2,512,1024]{2,1,0:T(8,128)} custom-call(f32[2,512,1024]{2,1,0:T(8,128)} %bitcast.3), custom_call_target="tpu_custom_call" | custom-call | tf_op jit(solution)/shard_map/pallas_call | solution.py:307
  179.2 4.8 %copy.3 = f32[1,2,512,1024]{3,2,1,0:T(8,128)} copy(f32[1,2,512,1024]{3,2,1,0:T(8,128)} %bitcast.2) | data formatting | bytes 8388608

commit v4 on v2

v4 whole, which is shorter than its diff:
```python
import functools

import jax
import jax.numpy as jnp
from jax import lax
from jax.experimental import pallas as pl
from jax.experimental.pallas import tpu as pltpu
from jax.sharding import PartitionSpec as P

MESH = pl.DeviceIdType.MESH
ROW_CHUNKS = 4
LANES = 128


def split(x):
    hi = x.astype(jnp.bfloat16)
    lo = (x - hi.astype(jnp.float32)).astype(jnp.bfloat16)
    return hi, lo


def kernel(
    n_col, x_ref, o_ref, a_land, b_land, b_hi, b_lo, lhs, acc, out_v,
    a_recv, a_right, a_left, ya_send, b_recv, yb_send, b_send, out_sem,
):
    T = ROW_CHUNKS
    rows, width = x_ref.shape[1], x_ref.shape[2]
    U = width // LANES
    V = U // 2
    half = rows // 2
    mt = half // T
    kw = width // 2
    cw = LANES

    sec, row, col = lax.axis_index("sec"), lax.axis_index("row"), lax.axis_index("col")
    parity = lax.rem(sec, 2)
    partner = {"sec": sec + 1 - 2 * parity}
    row1 = row + 1 - 2 * lax.rem(row, 2)
    row2 = row + 2 - 4 * lax.rem(lax.div(row, 2), 2)
    row3 = row1 + row2 - row
    has_left, has_right = col > 0, col < n_col - 1

    def remote(src, dst, send, recv, device):
        return pltpu.make_async_remote_copy(
            src_ref=src, dst_ref=dst, send_sem=send, recv_sem=recv,
            device_id=device, device_id_type=MESH,
        )

    def a_slot(j, t):
        return a_land.at[j, t]

    def a_rows(t, base):
        return x_ref.at[:, pl.ds(base + t * mt, mt), :]

    def b_cols(u):
        return pl.ds((u % 2) * kw + (u // 2) * cw, cw)

    def b_slot(who, u):
        return b_land.at[:, pl.ds(pl.multiple_of(who * rows, rows), rows), b_cols(u)]

    def right_copy(j, t):
        return remote(a_slot(j, t), a_slot(j, t), a_right.at[j, t], a_recv.at[j, t], {"col": col + 1})

    def left_copy(j, t):
        return remote(a_slot(j, t), a_slot(j, t), a_left.at[j, t], a_recv.at[j, t], {"col": col - 1})

    def ya_copy(t):
        return remote(a_rows(t, half), a_slot(col, t), ya_send.at[t], a_recv.at[col, t], partner)

    def yb_copy(u):
        return remote(
            x_ref.at[:, :, b_cols(u)], b_slot(row, u), yb_send.at[u], b_recv.at[0, u], partner
        )

    def b_copy(kind, u):
        who = row2 if kind == 2 else row
        device = {"row": row2} if kind == 1 else {"row": row1}
        return remote(
            b_slot(who, u), b_slot(who, u), b_send.at[kind, u], b_recv.at[kind + 1, u], device
        )

    def b_wait(kind, who, u):
        pltpu.make_async_copy(b_slot(who, u), b_slot(who, u), b_recv.at[kind, u]).wait()

    def convert(who, u):
        step = 64
        part = u % 2

        @pl.loop(0, rows // step)
        def _(i):
            at = pl.ds(pl.multiple_of(who * rows + i * step, step), step)
            hi, lo = split(b_land[:, at, b_cols(u)])
            b_hi[u // 2, :, at, part * cw:(part + 1) * cw] = hi
            b_lo[u // 2, :, at, part * cw:(part + 1) * cw] = lo

    def handle(j, t):
        pltpu.make_async_copy(a_slot(j, t), a_slot(j, t), a_recv.at[j, t]).wait()

        @pl.when(jnp.logical_and(j <= col, has_right))
        def _():
            right_copy(j, t).start()

        @pl.when(jnp.logical_and(j >= col, has_left))
        def _():
            left_copy(j, t).start()

    def a_tick(t, d):
        @pl.when(col >= d)
        def _():
            handle(col - d, t)

        @pl.when(col + d < n_col)
        def _():
            handle(col + d, t)

    def load(j, t):
        for mat in range(2):
            for part in range(2):
                at = pl.ds((2 * mat + part) * mt, mt)
                hi, lo = split(a_land[j, t, mat, :, part * kw:(part + 1) * kw])
                lhs[at, 0:kw] = hi
                lhs[at, kw:2 * kw] = hi
                lhs[at, 2 * kw:3 * kw] = lo

    def add(j, v):
        deep = pl.ds(pl.multiple_of(j * kw, kw), kw)
        rhs = []
        for mat in range(2):
            hi, lo = b_hi[v, mat, deep, :], b_lo[v, mat, deep, :]
            rhs.append(jnp.concatenate([hi, lo, hi], axis=0))
        acc[v] += jnp.dot(lhs[...], rhs[0], preferred_element_type=jnp.float32)
        acc[v, 2 * mt:4 * mt, :] += jnp.dot(
            lhs[0:2 * mt, :], rhs[1], preferred_element_type=jnp.float32
        )

    def out_at(t, v, part, base):
        return o_ref.at[
            :, pl.ds(pl.multiple_of(base + t * mt, mt), mt),
            pl.ds(pl.multiple_of(part * kw + v * cw, cw), cw),
        ]

    def out_from(t, v, part):
        return out_v.at[t, :, :, pl.ds(pl.multiple_of(part * kw + v * cw, cw), cw)]

    def out_remote(t, v, part):
        return remote(
            out_from(t, v, part), out_at(t, v, part, parity * half),
            out_sem.at[0, t, v, part], out_sem.at[1, t, v, part], partner,
        )

    def out_local(t, v, part):
        return pltpu.make_async_copy(
            out_from(t, v, part), out_at(t, v, part, parity * half), out_sem.at[2, t, v, part]
        )

    def finish(t, v):
        for mat in range(2):
            p = acc[v, 2 * mat * mt:(2 * mat + 1) * mt, :]
            q = acc[v, (2 * mat + 1) * mt:(2 * mat + 2) * mt, :]
            re, im = (pl.ds(pl.multiple_of(part * kw + v * cw, cw), cw) for part in range(2))
            out_v[t, mat, :, re] = p[:, 0:cw] - q[:, cw:]
            out_v[t, mat, :, im] = p[:, cw:] + q[:, 0:cw]
        for part in range(2):
            out_remote(t, v, part).start()
            out_local(t, v, part).start()

    def clear(v0, v1):
        @pl.loop(v0, v1)
        def _(v):
            acc[v] = jnp.zeros((4 * mt, 2 * cw), jnp.float32)

    def sum_block(t, v0, v1, reach):
        @pl.loop(0, 2 * reach + 1)
        def _(i):
            j = col + lax.div(i + 1, 2) * (1 - 2 * lax.rem(i, 2))

            @pl.when(jnp.logical_and(j >= 0, j < n_col))
            def _():
                load(j, t)

                @pl.loop(v0, v1)
                def _(v):
                    add(j, v)

    def block(t0, t1, v0, v1):
        @pl.loop(t0, t1)
        def _(t):
            clear(v0, v1)
            sum_block(t, v0, v1, n_col - 1)

            @pl.loop(v0, v1)
            def _(v):
                finish(t, v)

    barrier = pltpu.get_barrier_semaphore()
    for device in (partner, {"row": row1}, {"row": row2}):
        pl.semaphore_signal(barrier, inc=1, device_id=device, device_id_type=MESH)

    @pl.when(has_left)
    def _():
        pl.semaphore_signal(barrier, inc=1, device_id={"col": col - 1}, device_id_type=MESH)

    @pl.when(has_right)
    def _():
        pl.semaphore_signal(barrier, inc=1, device_id={"col": col + 1}, device_id_type=MESH)

    pl.semaphore_wait(barrier, 3 + has_left.astype(jnp.int32) + has_right.astype(jnp.int32))

    @pl.when(parity == 0)
    def _():
        for t in range(T):
            if t < 2:
                ya_copy(t).start()
            pltpu.make_async_copy(a_rows(t, 0), a_slot(col, t), a_recv.at[col, t]).start()

    @pl.when(parity == 1)
    def _():
        for u in range(U):
            if u < 3:
                yb_copy(u).start()
            pltpu.make_async_copy(
                x_ref.at[:, :, b_cols(u)], b_slot(row, u), b_recv.at[0, u]
            ).start()

    last = n_col - 1
    a_ticks = T * last

    def own_b(u):
        b_wait(0, row, u)
        b_copy(1, u).start()
        b_copy(0, u).start()

    @pl.when(parity == 1)
    def _():
        own_b(0)

    done = [0] * T
    for tick in range(max(a_ticks + 1, U + 2)):
        if tick < U:
            @pl.when(parity == 0)
            def _():
                own_b(tick)
        if tick + 1 < U:
            @pl.when(parity == 1)
            def _():
                own_b(tick + 1)
        for t in range(T):
            if tick == max(t * last - max(last - 1, 1), 0):
                handle(col, t)
        if tick < a_ticks - 1:
            @pl.when(parity == 0)
            def _():
                a_tick(tick // last, tick % last + 1)
        if tick == a_ticks:
            a_tick(T - 1, last)
        if 1 <= tick < a_ticks:
            @pl.when(parity == 1)
            def _():
                a_tick((tick - 1) // last, (tick - 1) % last + 1)
        if 1 <= tick < U + 1:
            b_wait(2, row2, tick - 1)
            b_copy(2, tick - 1).start()
        if tick + 3 < U:
            @pl.when(parity == 1)
            def _():
                yb_copy(tick).wait_send()
                yb_copy(tick + 3).start()
        if tick + 2 < T:
            @pl.when(parity == 0)
            def _():
                ya_copy(tick).wait_send()
                ya_copy(tick + 2).start()
        if tick < U:
            convert(row, tick)
        if 1 <= tick < U + 1:
            b_wait(1, row1, tick - 1)
            convert(row1, tick - 1)
            convert(row2, tick - 1)
        if 2 <= tick < U + 2:
            b_wait(3, row3, tick - 2)
            convert(row3, tick - 2)
        have = min(max((tick - 1) // 2, 0), V)
        t0 = 0
        while t0 < T - 1:
            t1 = t0 + 1
            if tick >= (t0 + 1) * last and done[t0] < have:
                while t1 < T - 1 and tick >= (t1 + 1) * last and done[t1] == done[t0]:
                    t1 += 1
                block(t0, t1, done[t0], have)
                done[t0:t1] = [have] * (t1 - t0)
            t0 = t1
        if tick == max(a_ticks - 1, U + 1):
            clear(0, V)
            sum_block(T - 1, 0, V, last - 1)

    @pl.when(jnp.logical_or(col == 0, col == last))
    def _():
        load(last - col, T - 1)

    @pl.loop(0, V)
    def _(v):
        @pl.when(jnp.logical_or(col == 0, col == last))
        def _():
            add(last - col, v)

        finish(T - 1, v)

    @pl.loop(0, T)
    def _(t):
        @pl.loop(0, V)
        def _(v):
            for part in range(2):
                out_local(t, v, part).wait()
                out_remote(t, v, part).wait_send()
                pltpu.make_async_copy(
                    out_from(t, v, part), out_at(t, v, part, (1 - parity) * half),
                    out_sem.at[1, t, v, part],
                ).wait()

    for kind in range(3):
        for u in range(U):
            b_copy(kind, u).wait_send()

    @pl.when(parity == 0)
    def _():
        for t in range(max(T - 2, 0), T):
            ya_copy(t).wait_send()

    @pl.when(parity == 1)
    def _():
        for u in range(max(U - 3, 0), U):
            yb_copy(u).wait_send()

    @pl.loop(0, n_col)
    def _(j):
        @pl.when(jnp.logical_and(j <= col, has_right))
        def _():
            for t in range(T):
                right_copy(j, t).wait_send()

        @pl.when(jnp.logical_and(j >= col, has_left))
        def _():
            for t in range(T):
                left_copy(j, t).wait_send()


def shards(n_row, n_col, pairs):
    _, _, rows, width = pairs.shape
    T = ROW_CHUNKS
    U = width // LANES
    mt = rows // 2 // T
    dma = pltpu.SemaphoreType.DMA
    combined = pl.pallas_call(
        functools.partial(kernel, n_col),
        out_shape=jax.ShapeDtypeStruct((2, rows, width), jnp.float32),
        in_specs=[pl.BlockSpec(memory_space=pl.ANY)],
        out_specs=pl.BlockSpec(memory_space=pl.ANY),
        scratch_shapes=[
            pltpu.VMEM((n_col, T, 2, mt, width), jnp.float32),
            pltpu.VMEM((2, n_row * rows, width), jnp.float32),
            pltpu.VMEM((U // 2, 2, n_row * rows, 2 * LANES), jnp.bfloat16),
            pltpu.VMEM((U // 2, 2, n_row * rows, 2 * LANES), jnp.bfloat16),
            pltpu.VMEM((4 * mt, 3 * width // 2), jnp.bfloat16),
            pltpu.VMEM((U // 2, 4 * mt, 2 * LANES), jnp.float32),
            pltpu.VMEM((T, 2, mt, width), jnp.float32),
            dma((n_col, T)),
            dma((n_col, T)),
            dma((n_col, T)),
            dma((T,)),
            dma((4, U)),
            dma((U,)),
            dma((3, U)),
            dma((3, T, U // 2, 2)),
        ],
        compiler_params=pltpu.CompilerParams(
            collective_id=0, has_side_effects=True, vmem_limit_bytes=58 * 1024 * 1024
        ),
    )(pairs[0])
    return combined[None]


def solution(mesh):
    spec = P("sec", None, "row", "col")
    return jax.shard_map(
        functools.partial(shards, mesh.shape["row"], mesh.shape["col"]),
        mesh=mesh, in_specs=(spec,), out_specs=spec, check_vma=False,
    )
```

time: 185 us -> 177 us (0.957)
  Pallas kernels: 180 us -> 172 us
    pallas_call x1, Pallas kernels: 180 us -> 172 us  [shards(): pl.pallas_call(functools.partial(kernel, n_col), out_shape=jax.ShapeDtype...]
where the time goes in v4:
time: 177 us
  Pallas kernels  172 us (97%)
  local copies, waits for them, and re-layouts  4.79 us (3%)
    pallas_call x1, Pallas kernels, shards(): pl.pallas_call(functools.partial(kernel, n_col), out_shape=jax.ShapeDtype...  172 us
    unnamed x1, local copies, waits for them, and re-layouts  4.79 us

profile of v4, /device:TPU:0, one launch (start us, length us, event | category | flops | bytes accessed | tf_op | source)
XLA Modules:
  0.0 176.5 jit_solution(4206136893634204259)
XLA Ops:
  0.0 171.7 %shard_map.17 = f32[2,512,1024]{2,1,0:T(8,128)} custom-call(f32[2,512,1024]{2,1,0:T(8,128)} %bitcast.3), custom_call_target="tpu_custom_call" | custom-call | tf_op jit(solution)/shard_map/pallas_call | solution.py:352
  171.7 4.8 %copy.3 = f32[1,2,512,1024]{3,2,1,0:T(8,128)} copy(f32[1,2,512,1024]{3,2,1,0:T(8,128)} %bitcast.2) | data formatting | bytes 8388608

commit v5 on v4

--- a/solution.py
+++ b/solution.py
@@ -103,14 +103,13 @@
         def _():
             left_copy(j, t).start()
 
-    def a_tick(t, d):
-        @pl.when(col >= d)
-        def _():
-            handle(col - d, t)
-
-        @pl.when(col + d < n_col)
-        def _():
-            handle(col + d, t)
+    def a_tick(e):
+        for count, sign in ((col, -1), (n_col - 1 - col, 1)):
+            @pl.when(jnp.logical_and(e >= 0, e < T * count))
+            def _():
+                n = jnp.maximum(count, 1)
+                t = lax.div(e, n)
+                handle(col + sign * (e - t * n + 1), t)
 
     def load(j, t):
         for mat in range(2):
@@ -160,8 +159,11 @@
             out_v[t, mat, :, re] = p[:, 0:cw] - q[:, cw:]
             out_v[t, mat, :, im] = p[:, cw:] + q[:, 0:cw]
         for part in range(2):
+            out_local(t, v, part).start()
+
+    def send(t, v):
+        for part in range(2):
             out_remote(t, v, part).start()
-            out_local(t, v, part).start()
 
     def clear(v0, v1):
         @pl.loop(v0, v1)
@@ -181,15 +183,19 @@
                 def _(v):
                     add(j, v)
 
-    def block(t0, t1, v0, v1):
-        @pl.loop(t0, t1)
-        def _(t):
-            clear(v0, v1)
-            sum_block(t, v0, v1, n_col - 1)
-
-            @pl.loop(v0, v1)
-            def _(v):
-                finish(t, v)
+    def block(t, v0, v1, hold):
+        clear(v0, v1)
+        sum_block(t, v0, v1, n_col - 1)
+
+        @pl.loop(v0, v1)
+        def _(v):
+            finish(t, v)
+            if hold:
+                @pl.when(parity == 0)
+                def _():
+                    send(t, v)
+            else:
+                send(t, v)
 
     barrier = pltpu.get_barrier_semaphore()
     for device in (partner, {"row": row1}, {"row": row2}):
@@ -233,7 +239,16 @@
     def _():
         own_b(0)
 
-    done = [0] * T
+    is_end = jnp.logical_or(col == 0, col == last)
+    incoming = jnp.maximum(col, last - col)
+    pace = jnp.minimum(col, last - col) + 1
+
+    def ready(t):
+        return (t + 1) * incoming - 1 + parity
+
+    def done_at(t, tick):
+        return jnp.where(ready(t) <= tick, min(max((tick - 1) // 2, 0), V), 0)
+
     for tick in range(max(a_ticks + 1, U + 2)):
         if tick < U:
             @pl.when(parity == 0)
@@ -244,18 +259,16 @@
             def _():
                 own_b(tick + 1)
         for t in range(T):
-            if tick == max(t * last - max(last - 1, 1), 0):
+            @pl.when(jnp.maximum(t * pace - 1 + parity, 0) == tick)
+            def _():
                 handle(col, t)
-        if tick < a_ticks - 1:
-            @pl.when(parity == 0)
-            def _():
-                a_tick(tick // last, tick % last + 1)
+        if tick < a_ticks:
+            e = tick - parity
+            if tick == a_ticks - 1:
+                e = jnp.where(parity == 0, -1, e)
+            a_tick(e)
         if tick == a_ticks:
-            a_tick(T - 1, last)
-        if 1 <= tick < a_ticks:
-            @pl.when(parity == 1)
-            def _():
-                a_tick((tick - 1) // last, (tick - 1) % last + 1)
+            a_tick(a_ticks - 1)
         if 1 <= tick < U + 1:
             b_wait(2, row2, tick - 1)
             b_copy(2, tick - 1).start()
@@ -278,31 +291,42 @@
         if 2 <= tick < U + 2:
             b_wait(3, row3, tick - 2)
             convert(row3, tick - 2)
-        have = min(max((tick - 1) // 2, 0), V)
-        t0 = 0
-        while t0 < T - 1:
-            t1 = t0 + 1
-            if tick >= (t0 + 1) * last and done[t0] < have:
-                while t1 < T - 1 and tick >= (t1 + 1) * last and done[t1] == done[t0]:
-                    t1 += 1
-                block(t0, t1, done[t0], have)
-                done[t0:t1] = [have] * (t1 - t0)
-            t0 = t1
+        if tick == U:
+            @pl.when(parity == 1)
+            def _():
+                for u in range(max(U - 3, 0), U):
+                    yb_copy(u).wait_send()
+
+                @pl.loop(0, T)
+                def _(t):
+                    @pl.loop(0, jnp.where(jnp.logical_and(is_end, t == T - 1), 0, done_at(t, tick - 1)))
+                    def _(v):
+                        send(t, v)
+
+        if tick >= 3:
+            @pl.loop(0, T - is_end.astype(jnp.int32))
+            def _(t):
+                v0, v1 = done_at(t, tick - 1), done_at(t, tick)
+
+                @pl.when(v1 > v0)
+                def _():
+                    block(t, v0, v1, tick < U)
+
         if tick == max(a_ticks - 1, U + 1):
-            clear(0, V)
-            sum_block(T - 1, 0, V, last - 1)
-
-    @pl.when(jnp.logical_or(col == 0, col == last))
+            @pl.when(is_end)
+            def _():
+                clear(0, V)
+                sum_block(T - 1, 0, V, last - 1)
+
+    @pl.when(is_end)
     def _():
         load(last - col, T - 1)
 
-    @pl.loop(0, V)
-    def _(v):
-        @pl.when(jnp.logical_or(col == 0, col == last))
-        def _():
+        @pl.loop(0, V)
+        def _(v):
             add(last - col, v)
-
-        finish(T - 1, v)
+            finish(T - 1, v)
+            send(T - 1, v)
 
     @pl.loop(0, T)
     def _(t):
@@ -324,11 +348,6 @@
     def _():
         for t in range(max(T - 2, 0), T):
             ya_copy(t).wait_send()
-
-    @pl.when(parity == 1)
-    def _():
-        for u in range(max(U - 3, 0), U):
-            yb_copy(u).wait_send()
 
     @pl.loop(0, n_col)
     def _(j):

time: 177 us -> 173 us (0.977)
  Pallas kernels: 172 us -> 168 us
    pallas_call x1, Pallas kernels: 172 us -> 168 us  [shards(): pl.pallas_call(functools.partial(kernel, n_col), out_shape=jax.ShapeDtype...]
where the time goes in v5:
time: 173 us
  Pallas kernels  168 us (97%)
  local copies, waits for them, and re-layouts  4.79 us (3%)
    pallas_call x1, Pallas kernels, shards(): pl.pallas_call(functools.partial(kernel, n_col), out_shape=jax.ShapeDtype...  168 us
    unnamed x1, local copies, waits for them, and re-layouts  4.79 us

profile of v5, /device:TPU:0, one launch (start us, length us, event | category | flops | bytes accessed | tf_op | source)
XLA Modules:
  0.0 172.6 jit_solution(11236190575724614595)
XLA Ops:
  0.0 167.8 %shard_map.17 = f32[2,512,1024]{2,1,0:T(8,128)} custom-call(f32[2,512,1024]{2,1,0:T(8,128)} %bitcast.3), custom_call_target="tpu_custom_call" | custom-call | tf_op jit(solution)/shard_map/pallas_call | solution.py:371
  167.8 4.8 %copy.3 = f32[1,2,512,1024]{3,2,1,0:T(8,128)} copy(f32[1,2,512,1024]{3,2,1,0:T(8,128)} %bitcast.2) | data formatting | bytes 8388608

commit v6 on v5

--- a/solution.py
+++ b/solution.py
@@ -19,7 +19,7 @@
 
 
 def kernel(
-    n_col, x_ref, o_ref, a_land, b_land, b_hi, b_lo, lhs, acc, out_v,
+    n_col, x_ref, o_ref, a_land, b_land, b_hi, b_lo, a_hi, a_lo, acc, out_v,
     a_recv, a_right, a_left, ya_send, b_recv, yb_send, b_send, out_sem,
 ):
     T = ROW_CHUNKS
@@ -116,19 +116,20 @@
             for part in range(2):
                 at = pl.ds((2 * mat + part) * mt, mt)
                 hi, lo = split(a_land[j, t, mat, :, part * kw:(part + 1) * kw])
-                lhs[at, 0:kw] = hi
-                lhs[at, kw:2 * kw] = hi
-                lhs[at, 2 * kw:3 * kw] = lo
-
-    def add(j, v):
+                a_hi[j, t, at, :] = hi
+                a_lo[j, t, at, :] = lo
+
+    def add(j, t, v):
         deep = pl.ds(pl.multiple_of(j * kw, kw), kw)
+        left_hi, left_lo = a_hi[j, t], a_lo[j, t]
+        lhs = jnp.concatenate([left_hi, left_hi, left_lo], axis=1)
         rhs = []
         for mat in range(2):
             hi, lo = b_hi[v, mat, deep, :], b_lo[v, mat, deep, :]
             rhs.append(jnp.concatenate([hi, lo, hi], axis=0))
-        acc[v] += jnp.dot(lhs[...], rhs[0], preferred_element_type=jnp.float32)
+        acc[v] += jnp.dot(lhs, rhs[0], preferred_element_type=jnp.float32)
         acc[v, 2 * mt:4 * mt, :] += jnp.dot(
-            lhs[0:2 * mt, :], rhs[1], preferred_element_type=jnp.float32
+            lhs[0:2 * mt], rhs[1], preferred_element_type=jnp.float32
         )
 
     def out_at(t, v, part, base):
@@ -177,11 +178,13 @@
 
             @pl.when(jnp.logical_and(j >= 0, j < n_col))
             def _():
-                load(j, t)
+                @pl.when(v0 == 0)
+                def _():
+                    load(j, t)
 
                 @pl.loop(v0, v1)
                 def _(v):
-                    add(j, v)
+                    add(j, t, v)
 
     def block(t, v0, v1, hold):
         clear(v0, v1)
@@ -214,7 +217,7 @@
     @pl.when(parity == 0)
     def _():
         for t in range(T):
-            if t < 2:
+            if t < 1:
                 ya_copy(t).start()
             pltpu.make_async_copy(a_rows(t, 0), a_slot(col, t), a_recv.at[col, t]).start()
 
@@ -258,10 +261,12 @@
             @pl.when(parity == 1)
             def _():
                 own_b(tick + 1)
-        for t in range(T):
-            @pl.when(jnp.maximum(t * pace - 1 + parity, 0) == tick)
-            def _():
-                handle(col, t)
+        own_t = lax.div(tick, pace)
+
+        @pl.when(jnp.logical_and(own_t * pace == tick, own_t < T))
+        def _():
+            handle(col, own_t)
+
         if tick < a_ticks:
             e = tick - parity
             if tick == a_ticks - 1:
@@ -277,11 +282,11 @@
             def _():
                 yb_copy(tick).wait_send()
                 yb_copy(tick + 3).start()
-        if tick + 2 < T:
+        if tick + 1 < T:
             @pl.when(parity == 0)
             def _():
                 ya_copy(tick).wait_send()
-                ya_copy(tick + 2).start()
+                ya_copy(tick + 1).start()
         if tick < U:
             convert(row, tick)
         if 1 <= tick < U + 1:
@@ -324,7 +329,7 @@
 
         @pl.loop(0, V)
         def _(v):
-            add(last - col, v)
+            add(last - col, T - 1, v)
             finish(T - 1, v)
             send(T - 1, v)
 
@@ -346,8 +351,7 @@
 
     @pl.when(parity == 0)
     def _():
-        for t in range(max(T - 2, 0), T):
-            ya_copy(t).wait_send()
+        ya_copy(T - 1).wait_send()
 
     @pl.loop(0, n_col)
     def _(j):
@@ -378,7 +382,8 @@
             pltpu.VMEM((2, n_row * rows, width), jnp.float32),
             pltpu.VMEM((U // 2, 2, n_row * rows, 2 * LANES), jnp.bfloat16),
             pltpu.VMEM((U // 2, 2, n_row * rows, 2 * LANES), jnp.bfloat16),
-            pltpu.VMEM((4 * mt, 3 * width // 2), jnp.bfloat16),
+            pltpu.VMEM((n_col, T, 4 * mt, width // 2), jnp.bfloat16),
+            pltpu.VMEM((n_col, T, 4 * mt, width // 2), jnp.bfloat16),
             pltpu.VMEM((U // 2, 4 * mt, 2 * LANES), jnp.float32),
             pltpu.VMEM((T, 2, mt, width), jnp.float32),
             dma((n_col, T)),

time: 173 us -> 172 us (level)
  no operation moved by 1% of the time
where the time goes in v6:
time: 172 us
  Pallas kernels  167 us (97%)
  local copies, waits for them, and re-layouts  4.79 us (3%)
    pallas_call x1, Pallas kernels, shards(): pl.pallas_call(functools.partial(kernel, n_col), out_shape=jax.ShapeDtype...  167 us
    unnamed x1, local copies, waits for them, and re-layouts  4.79 us

profile of v6, /device:TPU:0, one launch (start us, length us, event | category | flops | bytes accessed | tf_op | source)
XLA Modules:
  0.0 172.0 jit_solution(17090492067794783089)
XLA Ops:
  0.0 167.2 %shard_map.17 = f32[2,512,1024]{2,1,0:T(8,128)} custom-call(f32[2,512,1024]{2,1,0:T(8,128)} %bitcast.3), custom_call_target="tpu_custom_call" | custom-call | tf_op jit(solution)/shard_map/pallas_call | solution.py:375
  167.2 4.8 %copy.3 = f32[1,2,512,1024]{3,2,1,0:T(8,128)} copy(f32[1,2,512,1024]{3,2,1,0:T(8,128)} %bitcast.2) | data formatting | bytes 8388608
